TPU v7x, 256 devices: a whole 4x4x8 slice. The times are simulated.
256 devices in a mesh: ctx: 128 (over y, x, z), head: 2 (over core).
Axes of the slice: x: 4, y: 4, z: 8, core: 2. Of those that a mesh axis runs over, the one named last changes fastest.
Arguments:
- queries: bfloat16 [32768, 4096], P('ctx', 'head'), parts along dimension 1, may hold values from -3 to 3
- keys: bfloat16 [32768, 256], P('ctx', 'head'), parts along dimension 1, may hold values from -3 to 3
- values: bfloat16 [32768, 256], P('ctx', 'head'), parts along dimension 1, may hold values from -6 to 6
- outputs: bfloat16 [32768, 4096], P('ctx', 'head'), parts along dimension 1, may hold values from -3 to 3
- out_grad: bfloat16 [32768, 4096], P('ctx', 'head'), parts along dimension 1, may hold values from -1.1953125 to 1.1953125
- log_norm: float32 [16, 32768], P(None, 'ctx')
- doc_start: int32 [32768], P('ctx'), may hold values from 0 to 32767, as said below
Outputs:
- query_grad: float32 [32768, 4096], P('ctx', 'head'), parts along dimension 1
- key_grad: float32 [32768, 256], P('ctx', 'head'), parts along dimension 1
- value_grad: float32 [32768, 256], P('ctx', 'head'), parts along dimension 1
There are 2 independent parts, one for each index of `head`. A program takes and returns all parts, laid end to end along the dimension named above; an argument that names none is the same for every part. Nothing has to cross between parts.
Inputs may be any that keep to these rules, and one draw needn't show every extreme that they name: doc_start never falls and doc_start[t] <= t; documents are contiguous and hold at most 1536 tokens, some document exactly that many; the last token begins a document of its own.
All inputs are finite; a program needn't handle non-finite values.
Results may differ from a plain program's by a relative error of at most 0.0045.
Values may be sent and summed in bfloat16 or wider, within the bound.
A program may use at most 64 MiB of HBM per device.

v0:
```python
import jax
import jax.numpy as jnp
from jax import lax
from jax.sharding import PartitionSpec as P

REACH = 6


def shifted(x, axis, by):
    length = lax.axis_size(axis)
    pairs = [(i, i + by) for i in range(length) if 0 <= i + by < length]
    return lax.ppermute(x, axis, pairs)


def from_behind(x, axis, by):
    length = lax.axis_size(axis)
    return lax.ppermute(x, axis, [(i, (i + by) % length) for i in range(length)])


def tile_grads(query_side, row_stats, key_side, query_spots, key_spots):
    heads = (row_stats.shape[0] - 1) // 2
    tokens_here = query_side.shape[1]
    head_size = key_side.shape[2]
    factor = head_size ** (-0.5)
    queries = query_side[0].reshape(tokens_here, heads, head_size)
    out_grad = query_side[1].reshape(tokens_here, heads, head_size)
    log_norm = row_stats[:heads]
    out_dot = row_stats[heads : 2 * heads]
    starts = row_stats[2 * heads]
    scores = (
        jnp.einsum("thd,kd->htk", queries, key_side[0], preferred_element_type=jnp.float32) * factor
    )
    allowed = (key_spots[None, :] >= starts[:, None]) & (key_spots[None, :] <= query_spots[:, None])
    attention = jnp.where(allowed[None], jnp.exp(scores - log_norm[:, :, None]), 0.0)
    rounded = attention.astype(jnp.bfloat16)
    value_grad = jnp.einsum("htk,thd->kd", rounded, out_grad, preferred_element_type=jnp.float32)
    prob_grad = jnp.einsum("thd,kd->htk", out_grad, key_side[1], preferred_element_type=jnp.float32)
    score_grad = (attention * (prob_grad - out_dot[:, :, None])).astype(jnp.bfloat16)
    query_grad = jnp.einsum(
        "htk,kd->thd", score_grad, key_side[0], preferred_element_type=jnp.float32
    )
    query_grad = query_grad.reshape(tokens_here, heads * head_size) * factor
    key_grad = (
        jnp.einsum("htk,thd->kd", score_grad, queries, preferred_element_type=jnp.float32) * factor
    )
    return (query_grad, jnp.stack([key_grad, value_grad]))


def empty_grads(operands):
    query_side, row_stats, key_side, query_spots, key_spots = operands
    query_zero = jnp.zeros((query_side.shape[1], query_side.shape[2]), jnp.float32)
    key_zero = jnp.zeros(key_side.shape, jnp.float32)
    return (query_zero, key_zero)


def full_grads(operands):
    return tile_grads(*operands)


def attend(query_side, row_stats, key_side, query_spots, key_spots):
    heads = (row_stats.shape[0] - 1) // 2
    nonempty = (row_stats[2 * heads, 0] <= key_spots[-1]) & (key_spots[0] <= query_spots[-1])
    return lax.cond(
        nonempty, full_grads, empty_grads, (query_side, row_stats, key_side, query_spots, key_spots)
    )


def pass_keys(moved_keys, key_sums):
    moved_keys = shifted(moved_keys, "ctx", 1)
    key_sums = from_behind(key_sums, "ctx", 1)
    return (moved_keys, key_sums)


def keys_home(key_sums):
    return from_behind(key_sums, "ctx", -REACH)


def on_device(queries, keys, values, outputs, out_grad, log_norm, doc_start):
    row_count = keys.shape[0]
    head_count = log_norm.shape[0]
    head_size = keys.shape[1]
    shard_index = lax.axis_index("ctx")
    shard_count = lax.axis_size("ctx")
    spread = jnp.arange(row_count, dtype=jnp.int32)
    products = out_grad.astype(jnp.float32) * outputs.astype(jnp.float32)
    out_dot = jnp.sum(products.reshape(row_count, head_count, head_size), axis=2).T
    row_stats = jnp.concatenate([log_norm, out_dot, doc_start.astype(jnp.float32)[None, :]], axis=0)
    query_side = jnp.stack([queries, out_grad])
    key_side = jnp.stack([keys, values])

    def spots(offset):
        return ((shard_index + offset) % shard_count * row_count + spread).astype(jnp.float32)

    own_spots = spots(0)
    query_local, key_local = tile_grads(query_side, row_stats, key_side, own_spots, own_spots)

    def advance(offset, bundle):
        moved_keys, key_sums, query_here = bundle
        moved_keys, key_sums = pass_keys(moved_keys, key_sums)
        grad_query, grad_keys = attend(query_side, row_stats, moved_keys, own_spots, spots(-offset))
        return (moved_keys, key_sums + grad_keys, query_here + grad_query)

    bundle = lax.fori_loop(1, REACH + 1, advance, (key_side, key_local, query_local))
    query_grad = bundle[2]
    key_total = keys_home(bundle[1])
    return (query_grad, key_total[0], key_total[1])


def solution(mesh):
    placed = (
        P("ctx", "head"),
        P("ctx", "head"),
        P("ctx", "head"),
        P("ctx", "head"),
        P("ctx", "head"),
        P(None, "ctx"),
        P("ctx"),
    )
    return jax.shard_map(
        on_device,
        mesh=mesh,
        in_specs=placed,
        out_specs=(P("ctx", "head"), P("ctx", "head"), P("ctx", "head")),
        check_vma=False,
    )
```

profile of v0, /device:TPU:16, one launch (start us, length us, event | category | flops | bytes accessed | tf_op | source)
XLA Modules:
  0.0 175.7 jit_solution(11780310278658260724)
XLA Ops:
  8.2 2.7 %fusion.34 = bf16[16,256,256]{1,2,0:T(8,128)(2,1)S(1)} fusion(f32[256,256,16]{1,0,2:T(8,128)S(1)} %fusion.49, f32[16,256]{1,0:T(8,128)} %copy.31, f32[16,256]{1,0:T(8,128)} %param.16, pred[256,256]{0,1:T(8,128)(4,1)S(1)} %compare_and_fusion.1, bf16[256,128]{1,0:T(8,128)(2,1)S(1)} %copy-done.2, bf16[256,2048]{1,0:T(8,128)(2,1)} %param.15), kind=kOutput, calls=%fused_computation.38 | convolution fusion | flops 274726912 | bytes 7503872 | tf_op jit(solution)/shard_map/thd,kd->htk/dot_general | solution.py:37
  14.9 147.7 %while.20 = (s32[]{:T(128)}, bf16[2,256,128]{2,1,0:T(8,128)(2,1)}, f32[2,256,128]{2,1,0:T(8,128)}, f32[256,2048]{0,1:T(8,128)}, f32[1,256]{1,0:T(1,128)S(1)}, /*...) while((s32[]{:T(128)}, bf16[2,256,128]{2,1,0:T(8,128)(2,1)}, ...), condition=%wide.region_4.5_spmd.clone, body=%wide.region_1.4_spmd.clone.sunk | while | flops 1354072576 | bytes 35312136 | solution.py:103
  16.8 3.8 %collective-permute-start = (bf16[2,256,128]{2,1,0:T(8,128)(2,1)}, bf16[2,256,128]{2,1,0:T(8,128)(2,1)S(1)}, u32[]{:S(2)}, u32[]{:S(2)}) collective-permute-start(bf16[2,256,128]{2,1,0:T(8,128)(2,1)} %get-tuple-element.518), channel_id=1, source_target_pairs={{0,2},{2,4},{4,6},{6,8},{8,10},{10,12},{12,14},{14,16},{16,18},{18... | collective-permute-start | bytes 393224 | tf_op jit(solution)/shard_map/while/body/eval_jaxpr/ppermute | solution.py:12
  24.9 7.2 %collective-permute-done = bf16[2,256,128]{2,1,0:T(8,128)(2,1)S(1)} collective-permute-done((bf16[2,256,128]{2,1,0:T(8,128)(2,1)}, bf16[2,256,128]{2,1,0:T(8,128)(2,1)S(1)}, u32[]{:S(2)}, u32[]{:S(2)}) %collective-permute-start) | collective-permute-done | bytes 131104 | tf_op jit(solution)/shard_map/while/body/eval_jaxpr/ppermute | solution.py:12
  32.1 7.1 %conditional.3 = (f32[256,2048]{0,1:T(8,128)S(1)}, f32[2,256,128]{2,1,0:T(8,128)S(1)}) conditional(s32[]{:T(128)} %convert_element_type.77, () %tuple.62, (f32[256]{0:T(256)S(1)}, f32[256]{0:T(256)S(1)}, f32[256]{0:T(256)S(1)}, bf16[2,256,128]{2,1,0:T(8,128)(2,1)S(1)}, bf16[256,2048]{1,0:T(8,128)(2,1)S(1)}, /*index=5*/f32[16,256]{1,0:T(8,128)}, ...), branch_computations={%region_2.2_spmd, %region_3.3_spmd} | conditional | flops 1353482240 | bytes 26397712 | solution.py:63
  35.3 2.7 %fusion.3 = bf16[16,256,256]{1,2,0:T(8,128)(2,1)S(1)} fusion(f32[256,256,16]{1,0,2:T(8,128)S(1)} %fusion.18, f32[16,256]{1,0:T(8,128)} %get-tuple-element.317, f32[16,256]{1,0:T(8,128)} %get-tuple-element.315, pred[256,256]{0,1:T(8,128)(4,1)S(1)} %compare_and_fusion, bf16[2,256,128]{2,1,0:T(8,128)(2,1)S(1)} %get-tuple-element.313, ...), kind=kOutput, calls=%fused_computation.3 | convolution fusion | flops 274726912 | bytes 7503872 | tf_op jit(solution)/shard_map/while/body/eval_jaxpr/cond/branch_1_fun/thd,kd->htk/dot_general | solution.py:37
  39.3 3.2 %add.127 = f32[256,2048]{0,1:T(8,128)} add(f32[256,2048]{0,1:T(8,128)} %get-tuple-element.520, f32[256,2048]{0,1:T(8,128)S(1)} %get-tuple-element.495) | non-fusion elementwise | flops 524288 | bytes 6291456 | tf_op jit(solution)/shard_map/while/body/eval_jaxpr/add | solution.py:101
  51.0 8.6 %collective-permute-done = bf16[2,256,128]{2,1,0:T(8,128)(2,1)S(1)} collective-permute-done((bf16[2,256,128]{2,1,0:T(8,128)(2,1)}, bf16[2,256,128]{2,1,0:T(8,128)(2,1)S(1)}, u32[]{:S(2)}, u32[]{:S(2)}) %collective-permute-start) | collective-permute-done | bytes 131104 | tf_op jit(solution)/shard_map/while/body/eval_jaxpr/ppermute | solution.py:12
  59.6 7.1 %conditional.3 = (f32[256,2048]{0,1:T(8,128)S(1)}, f32[2,256,128]{2,1,0:T(8,128)S(1)}) conditional(s32[]{:T(128)} %convert_element_type.77, () %tuple.62, (f32[256]{0:T(256)S(1)}, f32[256]{0:T(256)S(1)}, f32[256]{0:T(256)S(1)}, bf16[2,256,128]{2,1,0:T(8,128)(2,1)S(1)}, bf16[256,2048]{1,0:T(8,128)(2,1)S(1)}, /*index=5*/f32[16,256]{1,0:T(8,128)}, ...), branch_computations={%region_2.2_spmd, %region_3.3_spmd} | conditional | flops 1353482240 | bytes 26397712 | solution.py:63
  62.7 2.7 %fusion.3 = bf16[16,256,256]{1,2,0:T(8,128)(2,1)S(1)} fusion(f32[256,256,16]{1,0,2:T(8,128)S(1)} %fusion.18, f32[16,256]{1,0:T(8,128)} %get-tuple-element.317, f32[16,256]{1,0:T(8,128)} %get-tuple-element.315, pred[256,256]{0,1:T(8,128)(4,1)S(1)} %compare_and_fusion, bf16[2,256,128]{2,1,0:T(8,128)(2,1)S(1)} %get-tuple-element.313, ...), kind=kOutput, calls=%fused_computation.3 | convolution fusion | flops 274726912 | bytes 7503872 | tf_op jit(solution)/shard_map/while/body/eval_jaxpr/cond/branch_1_fun/thd,kd->htk/dot_general | solution.py:37
  66.7 3.2 %add.127 = f32[256,2048]{0,1:T(8,128)} add(f32[256,2048]{0,1:T(8,128)} %get-tuple-element.520, f32[256,2048]{0,1:T(8,128)S(1)} %get-tuple-element.495) | non-fusion elementwise | flops 524288 | bytes 6291456 | tf_op jit(solution)/shard_map/while/body/eval_jaxpr/add | solution.py:101
  78.4 7.7 %collective-permute-done = bf16[2,256,128]{2,1,0:T(8,128)(2,1)S(1)} collective-permute-done((bf16[2,256,128]{2,1,0:T(8,128)(2,1)}, bf16[2,256,128]{2,1,0:T(8,128)(2,1)S(1)}, u32[]{:S(2)}, u32[]{:S(2)}) %collective-permute-start) | collective-permute-done | bytes 131104 | tf_op jit(solution)/shard_map/while/body/eval_jaxpr/ppermute | solution.py:12
  86.2 7.1 %conditional.3 = (f32[256,2048]{0,1:T(8,128)S(1)}, f32[2,256,128]{2,1,0:T(8,128)S(1)}) conditional(s32[]{:T(128)} %convert_element_type.77, () %tuple.62, (f32[256]{0:T(256)S(1)}, f32[256]{0:T(256)S(1)}, f32[256]{0:T(256)S(1)}, bf16[2,256,128]{2,1,0:T(8,128)(2,1)S(1)}, bf16[256,2048]{1,0:T(8,128)(2,1)S(1)}, /*index=5*/f32[16,256]{1,0:T(8,128)}, ...), branch_computations={%region_2.2_spmd, %region_3.3_spmd} | conditional | flops 1353482240 | bytes 26397712 | solution.py:63
  93.3 3.2 %add.127 = f32[256,2048]{0,1:T(8,128)} add(f32[256,2048]{0,1:T(8,128)} %get-tuple-element.520, f32[256,2048]{0,1:T(8,128)S(1)} %get-tuple-element.495) | non-fusion elementwise | flops 524288 | bytes 6291456 | tf_op jit(solution)/shard_map/while/body/eval_jaxpr/add | solution.py:101
  105.0 6.9 %collective-permute-done = bf16[2,256,128]{2,1,0:T(8,128)(2,1)S(1)} collective-permute-done((bf16[2,256,128]{2,1,0:T(8,128)(2,1)}, bf16[2,256,128]{2,1,0:T(8,128)(2,1)S(1)}, u32[]{:S(2)}, u32[]{:S(2)}) %collective-permute-start) | collective-permute-done | bytes 131104 | tf_op jit(solution)/shard_map/while/body/eval_jaxpr/ppermute | solution.py:12
  111.9 7.1 %conditional.3 = (f32[256,2048]{0,1:T(8,128)S(1)}, f32[2,256,128]{2,1,0:T(8,128)S(1)}) conditional(s32[]{:T(128)} %convert_element_type.77, () %tuple.62, (f32[256]{0:T(256)S(1)}, f32[256]{0:T(256)S(1)}, f32[256]{0:T(256)S(1)}, bf16[2,256,128]{2,1,0:T(8,128)(2,1)S(1)}, bf16[256,2048]{1,0:T(8,128)(2,1)S(1)}, /*index=5*/f32[16,256]{1,0:T(8,128)}, ...), branch_computations={%region_2.2_spmd, %region_3.3_spmd} | conditional | flops 1353482240 | bytes 26397712 | solution.py:63
  119.0 3.2 %add.127 = f32[256,2048]{0,1:T(8,128)} add(f32[256,2048]{0,1:T(8,128)} %get-tuple-element.520, f32[256,2048]{0,1:T(8,128)S(1)} %get-tuple-element.495) | non-fusion elementwise | flops 524288 | bytes 6291456 | tf_op jit(solution)/shard_map/while/body/eval_jaxpr/add | solution.py:101
  130.8 6.1 %collective-permute-done = bf16[2,256,128]{2,1,0:T(8,128)(2,1)S(1)} collective-permute-done((bf16[2,256,128]{2,1,0:T(8,128)(2,1)}, bf16[2,256,128]{2,1,0:T(8,128)(2,1)S(1)}, u32[]{:S(2)}, u32[]{:S(2)}) %collective-permute-start) | collective-permute-done | bytes 131104 | tf_op jit(solution)/shard_map/while/body/eval_jaxpr/ppermute | solution.py:12
  137.1 3.2 %add.127 = f32[256,2048]{0,1:T(8,128)} add(f32[256,2048]{0,1:T(8,128)} %get-tuple-element.520, f32[256,2048]{0,1:T(8,128)S(1)} %get-tuple-element.495) | non-fusion elementwise | flops 524288 | bytes 6291456 | tf_op jit(solution)/shard_map/while/body/eval_jaxpr/add | solution.py:101
  142.6 3.0 %collective-permute-start.1 = (f32[2,256,128]{2,1,0:T(8,128)}, f32[2,256,128]{2,1,0:T(8,128)}, u32[]{:S(2)}, u32[]{:S(2)}) collective-permute-start(f32[2,256,128]{2,1,0:T(8,128)} %get-tuple-element.519), channel_id=1, source_target_pairs={{0,2},{2,4},{4,6},{6,8},{8,10},{10,12},{12,14},{14,16},{16,18},{18... | collective-permute-start | bytes 786440 | tf_op jit(solution)/shard_map/while/body/eval_jaxpr/ppermute | solution.py:17
  151.8 5.1 %collective-permute-done = bf16[2,256,128]{2,1,0:T(8,128)(2,1)S(1)} collective-permute-done((bf16[2,256,128]{2,1,0:T(8,128)(2,1)}, bf16[2,256,128]{2,1,0:T(8,128)(2,1)S(1)}, u32[]{:S(2)}, u32[]{:S(2)}) %collective-permute-start) | collective-permute-done | bytes 131104 | tf_op jit(solution)/shard_map/while/body/eval_jaxpr/ppermute | solution.py:12
  157.1 3.2 %add.127 = f32[256,2048]{0,1:T(8,128)} add(f32[256,2048]{0,1:T(8,128)} %get-tuple-element.520, f32[256,2048]{0,1:T(8,128)S(1)} %get-tuple-element.495) | non-fusion elementwise | flops 524288 | bytes 6291456 | tf_op jit(solution)/shard_map/while/body/eval_jaxpr/add | solution.py:101
  162.6 2.9 %copy.37 = f32[256,2048]{1,0:T(8,128)} copy(f32[256,2048]{0,1:T(8,128)} %get-tuple-element.384) | data formatting | bytes 4194304
  165.5 9.4 %collective-permute-done.2 = f32[2,256,128]{2,1,0:T(8,128)S(1)} collective-permute-done((f32[2,256,128]{2,1,0:T(8,128)}, f32[2,256,128]{2,1,0:T(8,128)S(1)}, u32[]{:S(2)}, u32[]{:S(2)}) %collective-permute-start.2) | collective-permute-done | bytes 262176 | tf_op jit(solution)/shard_map/ppermute | solution.py:17
  (105 shorter events, 72.0 us)
Async XLA Ops:
  3.2 1.8 %copy-start = (bf16[256,2048]{1,0:T(8,128)(2,1)S(1)}, bf16[256,2048]{1,0:T(8,128)(2,1)}, u32[]{:S(2)}) copy-start(bf16[256,2048]{1,0:T(8,128)(2,1)} %param.11) | copy-start | bytes 3145732
  3.3 1.8 %copy-start.1 = (bf16[256,128]{1,0:T(8,128)(2,1)S(1)}, bf16[256,128]{1,0:T(8,128)(2,1)}, u32[]{:S(2)}) copy-start(bf16[256,128]{1,0:T(8,128)(2,1)} %param.12) | copy-start | bytes 196612
  5.8 2.4 %copy-start.2 = (bf16[256,128]{1,0:T(8,128)(2,1)S(1)}, bf16[256,128]{1,0:T(8,128)(2,1)}, u32[]{:S(2)}) copy-start(bf16[256,128]{1,0:T(8,128)(2,1)} %param.13) | copy-start | bytes 196612
  14.9 28.2 %collective-permute-start.1 = (f32[2,256,128]{2,1,0:T(8,128)}, f32[2,256,128]{2,1,0:T(8,128)}, u32[]{:S(2)}, u32[]{:S(2)}) collective-permute-start(f32[2,256,128]{2,1,0:T(8,128)} %get-tuple-element.519), channel_id=1, source_target_pairs={{0,2},{2,4},{4,6},{6,8},{8,10},{10,12},{12,14},{14,16},{16,18},{18... | collective-permute-start | bytes 786440 | tf_op jit(solution)/shard_map/while/body/eval_jaxpr/ppermute | solution.py:17
  16.8 15.4 %collective-permute-start = (bf16[2,256,128]{2,1,0:T(8,128)(2,1)}, bf16[2,256,128]{2,1,0:T(8,128)(2,1)S(1)}, u32[]{:S(2)}, u32[]{:S(2)}) collective-permute-start(bf16[2,256,128]{2,1,0:T(8,128)(2,1)} %get-tuple-element.518), channel_id=1, source_target_pairs={{0,2},{2,4},{4,6},{6,8},{8,10},{10,12},{12,14},{14,16},{16,18},{18... | collective-permute-start | bytes 393224 | tf_op jit(solution)/shard_map/while/body/eval_jaxpr/ppermute | solution.py:12
  44.8 25.7 %collective-permute-start.1 = (f32[2,256,128]{2,1,0:T(8,128)}, f32[2,256,128]{2,1,0:T(8,128)}, u32[]{:S(2)}, u32[]{:S(2)}) collective-permute-start(f32[2,256,128]{2,1,0:T(8,128)} %get-tuple-element.519), channel_id=1, source_target_pairs={{0,2},{2,4},{4,6},{6,8},{8,10},{10,12},{12,14},{14,16},{16,18},{18... | collective-permute-start | bytes 786440 | tf_op jit(solution)/shard_map/while/body/eval_jaxpr/ppermute | solution.py:17
  44.8 14.7 %collective-permute-start = (bf16[2,256,128]{2,1,0:T(8,128)(2,1)}, bf16[2,256,128]{2,1,0:T(8,128)(2,1)S(1)}, u32[]{:S(2)}, u32[]{:S(2)}) collective-permute-start(bf16[2,256,128]{2,1,0:T(8,128)(2,1)} %get-tuple-element.518), channel_id=1, source_target_pairs={{0,2},{2,4},{4,6},{6,8},{8,10},{10,12},{12,14},{14,16},{16,18},{18... | collective-permute-start | bytes 393224 | tf_op jit(solution)/shard_map/while/body/eval_jaxpr/ppermute | solution.py:12
  72.2 24.9 %collective-permute-start.1 = (f32[2,256,128]{2,1,0:T(8,128)}, f32[2,256,128]{2,1,0:T(8,128)}, u32[]{:S(2)}, u32[]{:S(2)}) collective-permute-start(f32[2,256,128]{2,1,0:T(8,128)} %get-tuple-element.519), channel_id=1, source_target_pairs={{0,2},{2,4},{4,6},{6,8},{8,10},{10,12},{12,14},{14,16},{16,18},{18... | collective-permute-start | bytes 786440 | tf_op jit(solution)/shard_map/while/body/eval_jaxpr/ppermute | solution.py:17
  72.2 13.9 %collective-permute-start = (bf16[2,256,128]{2,1,0:T(8,128)(2,1)}, bf16[2,256,128]{2,1,0:T(8,128)(2,1)S(1)}, u32[]{:S(2)}, u32[]{:S(2)}) collective-permute-start(bf16[2,256,128]{2,1,0:T(8,128)(2,1)} %get-tuple-element.518), channel_id=1, source_target_pairs={{0,2},{2,4},{4,6},{6,8},{8,10},{10,12},{12,14},{14,16},{16,18},{18... | collective-permute-start | bytes 393224 | tf_op jit(solution)/shard_map/while/body/eval_jaxpr/ppermute | solution.py:12
  98.8 24.1 %collective-permute-start.1 = (f32[2,256,128]{2,1,0:T(8,128)}, f32[2,256,128]{2,1,0:T(8,128)}, u32[]{:S(2)}, u32[]{:S(2)}) collective-permute-start(f32[2,256,128]{2,1,0:T(8,128)} %get-tuple-element.519), channel_id=1, source_target_pairs={{0,2},{2,4},{4,6},{6,8},{8,10},{10,12},{12,14},{14,16},{16,18},{18... | collective-permute-start | bytes 786440 | tf_op jit(solution)/shard_map/while/body/eval_jaxpr/ppermute | solution.py:17
  98.8 13.1 %collective-permute-start = (bf16[2,256,128]{2,1,0:T(8,128)(2,1)}, bf16[2,256,128]{2,1,0:T(8,128)(2,1)S(1)}, u32[]{:S(2)}, u32[]{:S(2)}) collective-permute-start(bf16[2,256,128]{2,1,0:T(8,128)(2,1)} %get-tuple-element.518), channel_id=1, source_target_pairs={{0,2},{2,4},{4,6},{6,8},{8,10},{10,12},{12,14},{14,16},{16,18},{18... | collective-permute-start | bytes 393224 | tf_op jit(solution)/shard_map/while/body/eval_jaxpr/ppermute | solution.py:12
  124.6 16.4 %collective-permute-start.1 = (f32[2,256,128]{2,1,0:T(8,128)}, f32[2,256,128]{2,1,0:T(8,128)}, u32[]{:S(2)}, u32[]{:S(2)}) collective-permute-start(f32[2,256,128]{2,1,0:T(8,128)} %get-tuple-element.519), channel_id=1, source_target_pairs={{0,2},{2,4},{4,6},{6,8},{8,10},{10,12},{12,14},{14,16},{16,18},{18... | collective-permute-start | bytes 786440 | tf_op jit(solution)/shard_map/while/body/eval_jaxpr/ppermute | solution.py:17
  124.6 12.3 %collective-permute-start = (bf16[2,256,128]{2,1,0:T(8,128)(2,1)}, bf16[2,256,128]{2,1,0:T(8,128)(2,1)S(1)}, u32[]{:S(2)}, u32[]{:S(2)}) collective-permute-start(bf16[2,256,128]{2,1,0:T(8,128)(2,1)} %get-tuple-element.518), channel_id=1, source_target_pairs={{0,2},{2,4},{4,6},{6,8},{8,10},{10,12},{12,14},{14,16},{16,18},{18... | collective-permute-start | bytes 393224 | tf_op jit(solution)/shard_map/while/body/eval_jaxpr/ppermute | solution.py:12
  142.6 18.3 %collective-permute-start.1 = (f32[2,256,128]{2,1,0:T(8,128)}, f32[2,256,128]{2,1,0:T(8,128)}, u32[]{:S(2)}, u32[]{:S(2)}) collective-permute-start(f32[2,256,128]{2,1,0:T(8,128)} %get-tuple-element.519), channel_id=1, source_target_pairs={{0,2},{2,4},{4,6},{6,8},{8,10},{10,12},{12,14},{14,16},{16,18},{18... | collective-permute-start | bytes 786440 | tf_op jit(solution)/shard_map/while/body/eval_jaxpr/ppermute | solution.py:17
  145.6 11.3 %collective-permute-start = (bf16[2,256,128]{2,1,0:T(8,128)(2,1)}, bf16[2,256,128]{2,1,0:T(8,128)(2,1)S(1)}, u32[]{:S(2)}, u32[]{:S(2)}) collective-permute-start(bf16[2,256,128]{2,1,0:T(8,128)(2,1)} %get-tuple-element.518), channel_id=1, source_target_pairs={{0,2},{2,4},{4,6},{6,8},{8,10},{10,12},{12,14},{14,16},{16,18},{18... | collective-permute-start | bytes 393224 | tf_op jit(solution)/shard_map/while/body/eval_jaxpr/ppermute | solution.py:12
  162.6 12.3 %collective-permute-start.2 = (f32[2,256,128]{2,1,0:T(8,128)}, f32[2,256,128]{2,1,0:T(8,128)S(1)}, u32[]{:S(2)}, u32[]{:S(2)}) collective-permute-start(f32[2,256,128]{2,1,0:T(8,128)} %get-tuple-element.340), channel_id=1, source_target_pairs={{0,244},{2,246},{4,248},{6,250},{8,252},{10,254},{12,0},{14,2},{16... | collective-permute-start | bytes 786440 | tf_op jit(solution)/shard_map/ppermute | solution.py:17
where the time goes:
time: 177 us; the launch traced here: 176 us
  waiting for transfers between devices  51.1 us (29%)
  matrix products  36.1 us (20%)
  other arithmetic  34.6 us (20%)
  local copies, waits for them, and re-layouts  19.7 us (11%)
  starting transfers between devices  18.3 us (10%)
  loops' own time  15.1 us (9%)
    ppermute x6, waiting for transfers between devices, shifted(): return lax.ppermute(x, axis, pairs)  41.6 us
    add x12, other arithmetic, advance(): return (moved_keys, key_sums + grad_keys, query_here + grad_query)  29.3 us
    another operation x1, loops' own time, on_device(): lax.fori_loop(1, REACH + 1, advance, (key_side, key_local, query_local))  14.9 us
    dot_general x5, matrix products, tile_grads(): jnp.einsum('thd,kd->htk', out_grad, key_side[1], preferred_element_type=j...  13.5 us
    ppermute x6, starting transfers between devices, shifted(): return lax.ppermute(x, axis, pairs)  13.4 us
    dot_general x5, matrix products, tile_grads(): jnp.einsum('htk,thd->kd', rounded, out_grad, preferred_element_type=jnp.f...  11.6 us
    ppermute x7, waiting for transfers between devices, from_behind(): lax.ppermute(x, axis, [(i, (i + by) % length) for i in range(length)])  9.46 us
    ppermute x7, starting transfers between devices, from_behind(): lax.ppermute(x, axis, [(i, (i + by) % length) for i in range(length)])  4.94 us
  transfers between devices with their start and end apart: 13, of which 7 were waited for; matrix products, arithmetic and copies ran while one was open for 37% of the time, Pallas kernels for 0%

commit v1 on v0

v1 whole, which is shorter than its diff:
```python
import functools

import jax
import jax.numpy as jnp
from jax import lax
from jax.experimental import pallas as pl
from jax.experimental.pallas import tpu as pltpu
from jax.sharding import PartitionSpec as P

MESH = pl.DeviceIdType.MESH
F32 = jnp.float32
BF16 = jnp.bfloat16
REACH = 6
LOG2E = 1.4426950408889634
AHEAD = 2
RELAY = 12


def dot(a, b, ca=1, cb=0):
    return lax.dot_general(a, b, (((ca,), (cb,)), ((), ())), preferred_element_type=F32)


def split(x, parts):
    out = []
    for _ in range(parts):
        piece = x.astype(BF16)
        out.append(piece)
        x = x - piece.astype(F32)
    return out


def kernel(
    n, q_hbm, k_hbm, v_hbm, o_hbm, g_hbm, norm_hbm, start_hbm, dq_hbm, dkv,
    q, g, o, qt, gt, norm, start, lnb, dotb, startb, bias, dq, kv, acc_in, acc_out,
    load_sem, store_sem, key_send, key_recv, acc_send, acc_recv,
):
    rows, width = q.shape
    d = kv.shape[3]
    heads = width // d
    half = rows // 2
    me = lax.axis_index("ctx")

    def at(offset):
        return {"ctx": lax.rem(me + (offset + n), n)}

    loads = [
        pltpu.make_async_copy(src, dst, load_sem.at[i])
        for i, (src, dst) in enumerate(
            [
                (k_hbm, kv.at[REACH, 0]),
                (v_hbm, kv.at[REACH, 1]),
                (norm_hbm, norm),
                (start_hbm, start),
                (q_hbm, q),
                (g_hbm, g),
                (o_hbm, o),
            ]
        )
    ]
    for c in loads:
        c.start()
    barrier = pltpu.get_barrier_semaphore()
    for offset in (1, -1, REACH, -REACH):
        pl.semaphore_signal(barrier, inc=1, device_id=at(offset), device_id_type=MESH)

    dq_store = pltpu.make_async_copy(dq, dq_hbm, store_sem)

    def key_copy(way, src, slot, offset):
        part = pl.ds(way * half, half)
        return pltpu.make_async_remote_copy(
            src_ref=kv.at[src, :, part],
            dst_ref=kv.at[slot, :, part],
            send_sem=key_send.at[way, slot],
            recv_sem=key_recv.at[way, slot],
            device_id=at(offset),
            device_id_type=MESH,
        )

    def acc_copy(way, s, offset):
        return pltpu.make_async_remote_copy(
            src_ref=acc_out.at[way, s],
            dst_ref=acc_in.at[way, s + 1],
            send_sem=acc_send.at[way, s],
            recv_sem=acc_recv.at[way, s + 1],
            device_id=at(offset),
            device_id_type=MESH,
        )

    loads[0].wait()
    loads[1].wait()
    pl.semaphore_wait(barrier, 4)
    key_copy(0, REACH, 0, 1).start()
    key_copy(1, REACH, 0, REACH).start()

    loads[2].wait()
    loads[3].wait()
    pieces = jnp.concatenate(split(norm[...] * LOG2E, 3), axis=0)
    row = lax.broadcasted_iota(jnp.int32, (3 * heads, width), 0)
    col = lax.broadcasted_iota(jnp.int32, (3 * heads, width), 1)
    pick = (col // d == row % heads).astype(F32).astype(BF16)
    lnb[...] = dot(pieces, pick, 0, 0)
    begins = jnp.broadcast_to(start[...].astype(F32), (16, rows))
    coarse = jnp.floor(begins * (1.0 / 256.0)) * 256.0
    line = lax.broadcasted_iota(jnp.int32, (16, rows), 0)
    begins = jnp.where(line == 0, coarse, jnp.where(line == 1, begins - coarse, 0.0))
    startb[...] = dot(begins.astype(BF16), jnp.ones((16, d), BF16), 0, 0)
    loads[4].wait()
    for h in range(heads):
        qt[h] = q[:, h * d : (h + 1) * d].T
    loads[5].wait()
    for h in range(heads):
        gt[h] = g[:, h * d : (h + 1) * d].T
    loads[6].wait()
    ones = jnp.ones((2 * d, d), BF16)
    for h in range(heads):
        cols = slice(h * d, (h + 1) * d)
        product = g[:, cols].astype(F32) * o[:, cols].astype(F32)
        dotb[:, cols] = dot(jnp.concatenate(split(product, 2), axis=1), ones)
    dq[...] = jnp.zeros_like(dq)
    acc_in[0, 0] = jnp.zeros_like(acc_in[0, 0])
    acc_in[1, 0] = jnp.zeros_like(acc_in[1, 0])

    key_copy(0, REACH, 0, 1).wait_recv()
    key_copy(1, REACH, 0, REACH).wait_recv()
    key_copy(0, 0, 1, 1).start()
    key_copy(1, 0, 1, -1).start()

    token = (me * rows).astype(F32) + lax.broadcasted_iota(jnp.int32, (rows, half), 0).astype(F32)
    lane = lax.broadcasted_iota(jnp.int32, (rows, half), 1).astype(F32)

    def step(s, _):
        own = s == REACH
        back = (jnp.where(own, 0, s + 1), REACH - s)
        begin = startb[...]
        for way in range(2):
            spot = ((me - back[way]) * rows + way * half).astype(F32) + lane
            allowed = (spot >= begin) & (spot <= token)
            bias[:, way * half : (way + 1) * half] = jnp.where(allowed, 0.0, -jnp.inf)
        k = kv[s, 0]
        v = kv[s, 1]

        def first(h):
            cols = slice(h * d, (h + 1) * d)
            return dot(q[:, cols], k, 1, 1), dot(g[:, cols], v, 1, 1)

        ready = [first(h) for h in range(AHEAD)]
        dk = jnp.zeros((d, rows), F32)
        dv = jnp.zeros((d, rows), F32)
        for h in range(heads):
            if h == RELAY:

                @pl.when(s < REACH - 1)
                def _():
                    key_copy(0, s, s + 1, 1).wait_recv()
                    key_copy(1, s, s + 1, -1).wait_recv()

                @pl.when(s < REACH - 2)
                def _():
                    key_copy(0, s + 1, s + 2, 1).start()
                    key_copy(1, s + 1, s + 2, -1).start()

            scores, prob_grad = ready.pop(0)
            if h + AHEAD < heads:
                ready.append(first(h + AHEAD))
            cols = slice(h * d, (h + 1) * d)
            shift = lnb[:, cols]
            shift = jnp.concatenate([shift, shift], axis=1)
            minus = dotb[:, cols]
            minus = jnp.concatenate([minus, minus], axis=1)
            attention = jnp.exp2(scores * (d**-0.5 * LOG2E) - shift + bias[...])
            score_grad = (attention * (prob_grad - minus)).astype(BF16)
            dv = dv + dot(gt[h], attention.astype(BF16))
            dk = dk + dot(qt[h], score_grad)
            dq[:, cols] += dot(score_grad, k)
        sums = (dk, dv)

        @pl.when(s == REACH)
        def _():
            dq_store.start()

        @pl.when(s > 0)
        def _():
            acc_copy(0, s - 1, 1).wait_recv()
            acc_copy(1, s - 1, -1).wait_recv()

        for way in range(2):
            cols = slice(way * half, (way + 1) * half)
            for i in range(2):
                total = sums[i][:, cols] + acc_in[way, s, i].astype(F32)
                dkv[i, :, cols] = total
                acc_out[way, s, i] = total.astype(BF16)

        @pl.when(s < REACH - 1)
        def _():
            acc_copy(0, s, 1).start()
            acc_copy(1, s, -1).start()

        @pl.when(s == REACH - 1)
        def _():
            acc_copy(0, s, -REACH).start()
            acc_copy(1, s, -1).start()

        return 0

    lax.fori_loop(0, REACH + 1, step, 0)
    dq_store.wait()

    def drain(s, _):
        for way in range(2):
            key_copy(way, REACH, s, 1).wait_send()
            acc_copy(way, s, 1).wait_send()
        return 0

    lax.fori_loop(0, REACH, drain, 0)


def on_device(n, queries, keys, values, outputs, out_grad, log_norm, doc_start):
    rows, width = queries.shape
    d = keys.shape[1]
    heads = width // d
    half = rows // 2
    anywhere = pl.BlockSpec(memory_space=pl.ANY)
    wide = pltpu.VMEM((rows, width), BF16)
    tall = pltpu.VMEM((heads, d, rows), BF16)
    full = pltpu.VMEM((rows, width), F32)
    copies = pltpu.SemaphoreType.DMA((2, REACH + 1))
    dq, dkv = pl.pallas_call(
        functools.partial(kernel, n),
        out_shape=(
            jax.ShapeDtypeStruct((rows, width), F32),
            jax.ShapeDtypeStruct((2, d, rows), F32),
        ),
        in_specs=[anywhere] * 7,
        out_specs=(anywhere, pl.BlockSpec(memory_space=pltpu.VMEM)),
        scratch_shapes=[
            wide, wide, wide, tall, tall,
            pltpu.VMEM((heads, rows), F32),
            pltpu.VMEM((1, rows), jnp.int32),
            full, full,
            pltpu.VMEM((rows, d), F32),
            pltpu.VMEM((rows, rows), F32),
            full,
            pltpu.VMEM((REACH + 1, 2, rows, d), BF16),
            pltpu.VMEM((2, REACH + 1, 2, d, half), BF16),
            pltpu.VMEM((2, REACH + 1, 2, d, half), BF16),
            pltpu.SemaphoreType.DMA((7,)),
            pltpu.SemaphoreType.DMA,
            copies, copies, copies, copies,
        ],
        compiler_params=pltpu.CompilerParams(
            collective_id=0, has_side_effects=True, vmem_limit_bytes=60 << 20
        ),
    )(queries, keys, values, outputs, out_grad, log_norm, doc_start.reshape(1, rows))
    factor = d**-0.5
    return dq * factor, dkv[0].T * factor, dkv[1].T


def solution(mesh):
    placed = (P("ctx", "head"),) * 5 + (P(None, "ctx"), P("ctx"))
    return jax.shard_map(
        functools.partial(on_device, mesh.shape["ctx"]),
        mesh=mesh,
        in_specs=placed,
        out_specs=(P("ctx", "head"),) * 3,
        check_vma=False,
    )
```

time: 177 us -> 64.3 us (0.36)
  the two profiles are of different devices: /device:TPU:16 before, /device:TPU:0 now
where the time goes in v1:
time: 64.3 us; the launch traced here: 64.2 us
  Pallas kernels  58.8 us (91%)
  other arithmetic  3.27 us (5%)
  local copies, waits for them, and re-layouts  1.51 us (2%)
  between operations  0.65 us (1%)
    pallas_call x1, Pallas kernels, on_device(): pl.pallas_call(functools.partial(kernel, n), out_shape=(jax.ShapeDtypeStr...  58.8 us
    mul x1, other arithmetic, on_device(): return (dq * factor, dkv[0].T * factor, dkv[1].T)  3.25 us
    unnamed x4, local copies, waits for them, and re-layouts  1.51 us

profile of v1, /device:TPU:0, one launch (start us, length us, event | category | flops | bytes accessed | tf_op | source)
XLA Modules:
  0.0 64.2 jit_solution(12398342988850413810)
XLA Ops:
  0.6 58.8 %shard_map.94 = (f32[256,2048]{1,0:T(8,128)}, f32[2,128,256]{2,1,0:T(8,128)}) custom-call(bf16[256,2048]{1,0:T(8,128)(2,1)} %q_hbm.1, bf16[256,128]{1,0:T(8,128)(2,1)} %k_hbm.1, bf16[256,128]{1,0:T(8,128)(2,1)} %v_hbm.1, bf16[256,2048]{1,0:T(8,128)(2,1)} %o_hbm.1, bf16[256,2048]{1,0:T(8,128)(2,1)} %g_hbm.1, f32[16,256]{1,0:T(8,128)} %norm_hbm.1, ...), custom_call_target="tpu_custom_call" | custom-call | tf_op jit(solution)/shard_map/pallas_call | solution.py:227
  59.4 0.0 copy-start
  59.4 3.2 %broadcast_multiply_fusion = f32[256,2048]{1,0:T(8,128)} fusion(f32[256,2048]{1,0:T(8,128)} %get-tuple-element.5), kind=kLoop, calls=%fused_computation | loop fusion | flops 524288 | bytes 4194304 | tf_op jit(solution)/shard_map/mul | solution.py:255
  62.7 0.0 copy-done
  62.7 0.8 %copy.11 = f32[256,128]{1,0:T(8,128)} copy(f32[256,128]{0,1:T(8,128)S(1)} %get-tuple-element.10) | data formatting | bytes 262144
  63.5 0.8 %copy.10 = f32[256,128]{1,0:T(8,128)} copy(f32[256,128]{0,1:T(8,128)S(1)} %get-tuple-element.11) | data formatting | bytes 262144
  (1 shorter events, 0.0 us)
Async XLA Ops:
  59.4 3.3 %copy-start = (f32[2,128,256]{2,1,0:T(8,128)S(1)}, f32[2,128,256]{2,1,0:T(8,128)}, u32[]{:S(2)}) copy-start(f32[2,128,256]{2,1,0:T(8,128)} %get-tuple-element.6) | copy-start | bytes 786436

commit v2 on v1

--- a/solution.py
+++ b/solution.py
@@ -47,8 +47,10 @@
         pltpu.make_async_copy(src, dst, load_sem.at[i])
         for i, (src, dst) in enumerate(
             [
-                (k_hbm, kv.at[REACH, 0]),
-                (v_hbm, kv.at[REACH, 1]),
+                (k_hbm.at[:half], kv.at[REACH, 0, :half]),
+                (v_hbm.at[:half], kv.at[REACH, 1, :half]),
+                (k_hbm.at[half:], kv.at[0, 0, half:]),
+                (v_hbm.at[half:], kv.at[0, 1, half:]),
                 (norm_hbm, norm),
                 (start_hbm, start),
                 (q_hbm, q),
@@ -86,14 +88,14 @@
             device_id_type=MESH,
         )
 
-    loads[0].wait()
-    loads[1].wait()
+    for c in loads[:4]:
+        c.wait()
     pl.semaphore_wait(barrier, 4)
     key_copy(0, REACH, 0, 1).start()
-    key_copy(1, REACH, 0, REACH).start()
-
-    loads[2].wait()
-    loads[3].wait()
+    key_copy(1, 0, 1, REACH).start()
+
+    loads[4].wait()
+    loads[5].wait()
     pieces = jnp.concatenate(split(norm[...] * LOG2E, 3), axis=0)
     row = lax.broadcasted_iota(jnp.int32, (3 * heads, width), 0)
     col = lax.broadcasted_iota(jnp.int32, (3 * heads, width), 1)
@@ -104,33 +106,30 @@
     line = lax.broadcasted_iota(jnp.int32, (16, rows), 0)
     begins = jnp.where(line == 0, coarse, jnp.where(line == 1, begins - coarse, 0.0))
     startb[...] = dot(begins.astype(BF16), jnp.ones((16, d), BF16), 0, 0)
-    loads[4].wait()
+    loads[6].wait()
     for h in range(heads):
         qt[h] = q[:, h * d : (h + 1) * d].T
-    loads[5].wait()
+    loads[7].wait()
     for h in range(heads):
         gt[h] = g[:, h * d : (h + 1) * d].T
-    loads[6].wait()
+    loads[8].wait()
     ones = jnp.ones((2 * d, d), BF16)
     for h in range(heads):
         cols = slice(h * d, (h + 1) * d)
         product = g[:, cols].astype(F32) * o[:, cols].astype(F32)
         dotb[:, cols] = dot(jnp.concatenate(split(product, 2), axis=1), ones)
     dq[...] = jnp.zeros_like(dq)
-    acc_in[0, 0] = jnp.zeros_like(acc_in[0, 0])
-    acc_in[1, 0] = jnp.zeros_like(acc_in[1, 0])
+    for way, slot in ((0, 0), (1, 0), (1, 1)):
+        acc_in[way, slot] = jnp.zeros_like(acc_in[way, slot])
 
     key_copy(0, REACH, 0, 1).wait_recv()
-    key_copy(1, REACH, 0, REACH).wait_recv()
     key_copy(0, 0, 1, 1).start()
-    key_copy(1, 0, 1, -1).start()
 
     token = (me * rows).astype(F32) + lax.broadcasted_iota(jnp.int32, (rows, half), 0).astype(F32)
     lane = lax.broadcasted_iota(jnp.int32, (rows, half), 1).astype(F32)
 
     def step(s, _):
-        own = s == REACH
-        back = (jnp.where(own, 0, s + 1), REACH - s)
+        back = (jnp.where(s == REACH, 0, s + 1), jnp.where(s == 0, 0, REACH + 1 - s))
         begin = startb[...]
         for way in range(2):
             spot = ((me - back[way]) * rows + way * half).astype(F32) + lane
@@ -152,11 +151,17 @@
                 @pl.when(s < REACH - 1)
                 def _():
                     key_copy(0, s, s + 1, 1).wait_recv()
-                    key_copy(1, s, s + 1, -1).wait_recv()
 
                 @pl.when(s < REACH - 2)
                 def _():
                     key_copy(0, s + 1, s + 2, 1).start()
+
+                @pl.when(s < REACH)
+                def _():
+                    key_copy(1, s, s + 1, -1).wait_recv()
+
+                @pl.when(s < REACH - 1)
+                def _():
                     key_copy(1, s + 1, s + 2, -1).start()
 
             scores, prob_grad = ready.pop(0)
@@ -178,40 +183,77 @@
         def _():
             dq_store.start()
 
-        @pl.when(s > 0)
-        def _():
-            acc_copy(0, s - 1, 1).wait_recv()
-            acc_copy(1, s - 1, -1).wait_recv()
-
-        for way in range(2):
+        def finish(way):
             cols = slice(way * half, (way + 1) * half)
             for i in range(2):
                 total = sums[i][:, cols] + acc_in[way, s, i].astype(F32)
+                acc_out[way, s, i] = total.astype(BF16)
+                yield i, cols, total
+
+        @pl.when(s > 0)
+        def _():
+            acc_copy(0, s - 1, 1).wait_recv()
+
+        for i, cols, total in finish(0):
+            dkv[i, :, cols] = total
+
+        @pl.when(s < REACH - 1)
+        def _():
+            acc_copy(0, s, 1).start()
+
+        @pl.when(s == REACH - 1)
+        def _():
+            acc_copy(0, s, -REACH).start()
+
+        @pl.when(s > 1)
+        def _():
+            acc_copy(1, s - 1, -1).wait_recv()
+
+        for i, cols, total in finish(1):
+
+            @pl.when(s == 0)
+            def _():
                 dkv[i, :, cols] = total
-                acc_out[way, s, i] = total.astype(BF16)
-
-        @pl.when(s < REACH - 1)
-        def _():
-            acc_copy(0, s, 1).start()
+
+        @pl.when(s > 0)
+        def _():
             acc_copy(1, s, -1).start()
 
-        @pl.when(s == REACH - 1)
-        def _():
-            acc_copy(0, s, -REACH).start()
-            acc_copy(1, s, -1).start()
-
         return 0
 
     lax.fori_loop(0, REACH + 1, step, 0)
+    acc_copy(1, REACH, -1).wait_recv()
+    dkv[:, :, half:] += acc_in[1, REACH + 1].astype(F32)
     dq_store.wait()
 
     def drain(s, _):
         for way in range(2):
-            key_copy(way, REACH, s, 1).wait_send()
-            acc_copy(way, s, 1).wait_send()
+            key_copy(way, REACH, s + way, 1).wait_send()
+            acc_copy(way, s + way, 1).wait_send()
         return 0
 
     lax.fori_loop(0, REACH, drain, 0)
+
+
+def finish_kernel(dq_ref, dkv_ref, dq_hbm, dk_hbm, dv_hbm, dq, dk, dv, sems):
+    rows, width = dq.shape
+    factor = dk.shape[1] ** -0.5
+    dk[...] = dkv_ref[0].T * factor
+    dv[...] = dkv_ref[1].T
+    copies = [
+        pltpu.make_async_copy(dk, dk_hbm, sems.at[0]),
+        pltpu.make_async_copy(dv, dv_hbm, sems.at[1]),
+    ]
+    for c in copies:
+        c.start()
+    part = rows // 4
+    for i in range(4):
+        here = pl.ds(i * part, part)
+        dq[here, :] = dq_ref[here, :] * factor
+        copies.append(pltpu.make_async_copy(dq.at[here], dq_hbm.at[here], sems.at[2 + i]))
+        copies[-1].start()
+    for c in copies:
+        c.wait()
 
 
 def on_device(n, queries, keys, values, outputs, out_grad, log_norm, doc_start):
@@ -223,13 +265,10 @@
     wide = pltpu.VMEM((rows, width), BF16)
     tall = pltpu.VMEM((heads, d, rows), BF16)
     full = pltpu.VMEM((rows, width), F32)
-    copies = pltpu.SemaphoreType.DMA((2, REACH + 1))
+    copies = pltpu.SemaphoreType.DMA((2, REACH + 2))
     dq, dkv = pl.pallas_call(
         functools.partial(kernel, n),
-        out_shape=(
-            jax.ShapeDtypeStruct((rows, width), F32),
-            jax.ShapeDtypeStruct((2, d, rows), F32),
-        ),
+        out_shape=(pltpu.VMEM((rows, width), F32), pltpu.VMEM((2, d, rows), F32)),
         in_specs=[anywhere] * 7,
         out_specs=(anywhere, pl.BlockSpec(memory_space=pltpu.VMEM)),
         scratch_shapes=[
@@ -241,18 +280,31 @@
             pltpu.VMEM((rows, rows), F32),
             full,
             pltpu.VMEM((REACH + 1, 2, rows, d), BF16),
+            pltpu.VMEM((2, REACH + 2, 2, d, half), BF16),
             pltpu.VMEM((2, REACH + 1, 2, d, half), BF16),
-            pltpu.VMEM((2, REACH + 1, 2, d, half), BF16),
-            pltpu.SemaphoreType.DMA((7,)),
+            pltpu.SemaphoreType.DMA((9,)),
             pltpu.SemaphoreType.DMA,
             copies, copies, copies, copies,
         ],
         compiler_params=pltpu.CompilerParams(
-            collective_id=0, has_side_effects=True, vmem_limit_bytes=60 << 20
+            collective_id=0, has_side_effects=True, vmem_limit_bytes=56 << 20
         ),
     )(queries, keys, values, outputs, out_grad, log_norm, doc_start.reshape(1, rows))
-    factor = d**-0.5
-    return dq * factor, dkv[0].T * factor, dkv[1].T
+    whole = pl.BlockSpec(memory_space=pltpu.VMEM)
+    square = jax.ShapeDtypeStruct((rows, d), F32)
+    return pl.pallas_call(
+        finish_kernel,
+        out_shape=(jax.ShapeDtypeStruct((rows, width), F32), square, square),
+        in_specs=[whole, whole],
+        out_specs=(anywhere,) * 3,
+        scratch_shapes=[
+            full,
+            pltpu.VMEM((rows, d), F32),
+            pltpu.VMEM((rows, d), F32),
+            pltpu.SemaphoreType.DMA((6,)),
+        ],
+        compiler_params=pltpu.CompilerParams(vmem_limit_bytes=16 << 20),
+    )(dq, dkv)
 
 
 def solution(mesh):

time: 64.3 us -> 54.7 us (0.85)
  the two profiles are of different devices: /device:TPU:0 before, /device:TPU:62 now
where the time goes in v2:
time: 54.7 us
  Pallas kernels  54 us (99%)
  between operations  0.64 us (1%)
    pallas_call x1, Pallas kernels, on_device(): pl.pallas_call(functools.partial(kernel, n), out_shape=(pltpu.VMEM((rows,...  52.5 us
    pallas_call x1, Pallas kernels, on_device(): pl.pallas_call(finish_kernel, out_shape=(jax.ShapeDtypeStruct((rows, widt...  1.55 us

profile of v2, /device:TPU:62, one launch (start us, length us, event | category | flops | bytes accessed | tf_op | source)
XLA Modules:
  0.0 54.7 jit_solution(8762623664470208194)
XLA Ops:
  0.6 52.5 %shard_map.94 = (f32[256,2048]{1,0:T(8,128)S(1)}, f32[2,128,256]{2,1,0:T(8,128)S(1)}) custom-call(bf16[256,2048]{1,0:T(8,128)(2,1)} %q_hbm.1, bf16[256,128]{1,0:T(8,128)(2,1)} %k_hbm.1, bf16[256,128]{1,0:T(8,128)(2,1)} %v_hbm.1, bf16[256,2048]{1,0:T(8,128)(2,1)} %o_hbm.1, bf16[256,2048]{1,0:T(8,128)(2,1)} %g_hbm.1, f32[16,256]{1,0:T(8,128)} %norm_hbm.1, ...), custom_call_target="tpu_custom_call" | custom-call | tf_op jit(solution)/shard_map/pallas_call | solution.py:269
  53.1 1.6 %shard_map.95 = (f32[256,2048]{1,0:T(8,128)}, f32[256,128]{1,0:T(8,128)}, f32[256,128]{1,0:T(8,128)}) custom-call(f32[256,2048]{1,0:T(8,128)S(1)} %get-tuple-element.5.dq_ref, f32[2,128,256]{2,1,0:T(8,128)S(1)} %get-tuple-element.6.dkv_ref), custom_call_target="tpu_custom_call" | custom-call | tf_op jit(solution)/shard_map/pallas_call | solution.py:295

commit v3 on v2

--- a/solution.py
+++ b/solution.py
@@ -13,7 +13,8 @@
 REACH = 6
 LOG2E = 1.4426950408889634
 AHEAD = 2
-RELAY = 12
+RELAY = (12, 12)
+LATE = 8
 
 
 def dot(a, b, ca=1, cb=0):
@@ -31,26 +32,49 @@
 
 def kernel(
     n, q_hbm, k_hbm, v_hbm, o_hbm, g_hbm, norm_hbm, start_hbm, dq_hbm, dkv,
-    q, g, o, qt, gt, norm, start, lnb, dotb, startb, bias, dq, kv, acc_in, acc_out,
+    q, g, o, qt, gt, norm, start, lnb, dotb, startb, bias, dq, kv, acc_in, acc_out, later,
     load_sem, store_sem, key_send, key_recv, acc_send, acc_recv,
 ):
     rows, width = q.shape
-    d = kv.shape[3]
+    d = kv.shape[4]
     heads = width // d
     half = rows // 2
     me = lax.axis_index("ctx")
 
     def at(offset):
         return {"ctx": lax.rem(me + (offset + n), n)}
+
+    last = me == n - 1
+
+    @pl.when(me < REACH)
+    def _():
+        kv[...] = jnp.zeros_like(kv)
+
+    acc_in[...] = jnp.zeros_like(acc_in)
+    barrier = pltpu.get_barrier_semaphore()
+
+    peers = jnp.int32(0)
+
+    def greet(offset, meets):
+        @pl.when(meets)
+        def _():
+            pl.semaphore_signal(barrier, inc=1, device_id=at(offset), device_id_type=MESH)
+
+        return jnp.where(meets, 1, 0)
+
+    for offset in (1, -1, REACH, -REACH):
+        peers = peers + greet(offset, (me + offset >= 0) & (me + offset < n))
+    for offset in range(2, REACH):
+        peers = peers + greet(offset, me == n - 1 - offset) + greet(-offset, last)
 
     loads = [
         pltpu.make_async_copy(src, dst, load_sem.at[i])
         for i, (src, dst) in enumerate(
             [
-                (k_hbm.at[:half], kv.at[REACH, 0, :half]),
-                (v_hbm.at[:half], kv.at[REACH, 1, :half]),
-                (k_hbm.at[half:], kv.at[0, 0, half:]),
-                (v_hbm.at[half:], kv.at[0, 1, half:]),
+                (k_hbm.at[:half], kv.at[REACH, 0, 0]),
+                (v_hbm.at[:half], kv.at[REACH, 0, 1]),
+                (k_hbm.at[half:], kv.at[0, 1, 0]),
+                (v_hbm.at[half:], kv.at[0, 1, 1]),
                 (norm_hbm, norm),
                 (start_hbm, start),
                 (q_hbm, q),
@@ -61,17 +85,12 @@
     ]
     for c in loads:
         c.start()
-    barrier = pltpu.get_barrier_semaphore()
-    for offset in (1, -1, REACH, -REACH):
-        pl.semaphore_signal(barrier, inc=1, device_id=at(offset), device_id_type=MESH)
-
     dq_store = pltpu.make_async_copy(dq, dq_hbm, store_sem)
 
     def key_copy(way, src, slot, offset):
-        part = pl.ds(way * half, half)
         return pltpu.make_async_remote_copy(
-            src_ref=kv.at[src, :, part],
-            dst_ref=kv.at[slot, :, part],
+            src_ref=kv.at[src, way],
+            dst_ref=kv.at[slot, way],
             send_sem=key_send.at[way, slot],
             recv_sem=key_recv.at[way, slot],
             device_id=at(offset),
@@ -88,11 +107,43 @@
             device_id_type=MESH,
         )
 
+    def own_send(slot, offset):
+        return pltpu.make_async_remote_copy(
+            src_ref=kv.at[0, 1],
+            dst_ref=kv.at[slot, 1],
+            send_sem=key_send.at[1, 0],
+            recv_sem=key_recv.at[1, slot],
+            device_id=at(offset),
+            device_id_type=MESH,
+        )
+
+    def acc_home(s):
+        return pltpu.make_async_remote_copy(
+            src_ref=acc_out.at[0, s],
+            dst_ref=acc_in.at[0, REACH],
+            send_sem=acc_send.at[0, s],
+            recv_sem=acc_recv.at[0, REACH],
+            device_id=at(-1 - s),
+            device_id_type=MESH,
+        )
+
     for c in loads[:4]:
         c.wait()
-    pl.semaphore_wait(barrier, 4)
-    key_copy(0, REACH, 0, 1).start()
-    key_copy(1, 0, 1, REACH).start()
+    pl.semaphore_wait(barrier, peers)
+
+    @pl.when(me < n - 1)
+    def _():
+        key_copy(0, REACH, 0, 1).start()
+
+    @pl.when(me < n - REACH)
+    def _():
+        key_copy(1, 0, 1, REACH).start()
+
+    for offset in range(1, REACH):
+
+        @pl.when(me == n - 1 - offset)
+        def _():
+            own_send(REACH + 1 - offset, offset).start()
 
     loads[4].wait()
     loads[5].wait()
@@ -119,14 +170,28 @@
         product = g[:, cols].astype(F32) * o[:, cols].astype(F32)
         dotb[:, cols] = dot(jnp.concatenate(split(product, 2), axis=1), ones)
     dq[...] = jnp.zeros_like(dq)
-    for way, slot in ((0, 0), (1, 0), (1, 1)):
-        acc_in[way, slot] = jnp.zeros_like(acc_in[way, slot])
-
-    key_copy(0, REACH, 0, 1).wait_recv()
-    key_copy(0, 0, 1, 1).start()
+
+    @pl.when(me > 0)
+    def _():
+        key_copy(0, REACH, 0, 1).wait_recv()
+
+    @pl.when((me > 0) & (me < n - 1))
+    def _():
+        key_copy(0, 0, 1, 1).start()
 
     token = (me * rows).astype(F32) + lax.broadcasted_iota(jnp.int32, (rows, half), 0).astype(F32)
     lane = lax.broadcasted_iota(jnp.int32, (rows, half), 1).astype(F32)
+
+    def pass_on(s):
+        @pl.when((s > 1) & (me >= REACH + 1 - s) & (me < n - 1))
+        def _():
+            acc_copy(1, s - 1, -1).wait_recv()
+
+        acc_out[1, s] = (later[...] + acc_in[1, s].astype(F32)).astype(BF16)
+
+        @pl.when(me >= REACH + 1 - s)
+        def _():
+            acc_copy(1, s, -1).start()
 
     def step(s, _):
         back = (jnp.where(s == REACH, 0, s + 1), jnp.where(s == 0, 0, REACH + 1 - s))
@@ -135,8 +200,8 @@
             spot = ((me - back[way]) * rows + way * half).astype(F32) + lane
             allowed = (spot >= begin) & (spot <= token)
             bias[:, way * half : (way + 1) * half] = jnp.where(allowed, 0.0, -jnp.inf)
-        k = kv[s, 0]
-        v = kv[s, 1]
+        k = jnp.concatenate([kv[s, 0, 0], kv[s, 1, 0]], axis=0)
+        v = jnp.concatenate([kv[s, 0, 1], kv[s, 1, 1]], axis=0)
 
         def first(h):
             cols = slice(h * d, (h + 1) * d)
@@ -146,23 +211,31 @@
         dk = jnp.zeros((d, rows), F32)
         dv = jnp.zeros((d, rows), F32)
         for h in range(heads):
-            if h == RELAY:
-
-                @pl.when(s < REACH - 1)
+            if h == RELAY[0]:
+
+                @pl.when((s < REACH - 1) & (me > s + 1))
                 def _():
                     key_copy(0, s, s + 1, 1).wait_recv()
 
-                @pl.when(s < REACH - 2)
+                @pl.when((s < REACH - 2) & (me > s + 1) & (me < n - 1))
                 def _():
                     key_copy(0, s + 1, s + 2, 1).start()
 
-                @pl.when(s < REACH)
+            if h == RELAY[1]:
+
+                @pl.when((s < REACH) & (me >= REACH - s))
                 def _():
                     key_copy(1, s, s + 1, -1).wait_recv()
 
-                @pl.when(s < REACH - 1)
+                @pl.when((s < REACH - 1) & (me >= REACH - s))
                 def _():
                     key_copy(1, s + 1, s + 2, -1).start()
+
+            if h == LATE:
+
+                @pl.when(s > 1)
+                def _():
+                    pass_on(s - 1)
 
             scores, prob_grad = ready.pop(0)
             if h + AHEAD < heads:
@@ -183,54 +256,68 @@
         def _():
             dq_store.start()
 
-        def finish(way):
-            cols = slice(way * half, (way + 1) * half)
-            for i in range(2):
-                total = sums[i][:, cols] + acc_in[way, s, i].astype(F32)
-                acc_out[way, s, i] = total.astype(BF16)
-                yield i, cols, total
-
-        @pl.when(s > 0)
+        @pl.when((s > 0) & (((s < REACH) & (me > s)) | ((s == REACH) & (me < n - 1))))
         def _():
             acc_copy(0, s - 1, 1).wait_recv()
 
-        for i, cols, total in finish(0):
-            dkv[i, :, cols] = total
-
-        @pl.when(s < REACH - 1)
+        for i in range(2):
+            total = sums[i][:, :half] + acc_in[0, s, i].astype(F32)
+            dkv[i, :, :half] = total
+            acc_out[0, s, i] = total.astype(BF16)
+            later[i] = sums[i][:, half:]
+
+        @pl.when((s < REACH - 1) & (me > s) & (me < n - 1))
         def _():
             acc_copy(0, s, 1).start()
 
-        @pl.when(s == REACH - 1)
-        def _():
-            acc_copy(0, s, -REACH).start()
-
-        @pl.when(s > 1)
-        def _():
-            acc_copy(1, s - 1, -1).wait_recv()
-
-        for i, cols, total in finish(1):
-
-            @pl.when(s == 0)
-            def _():
-                dkv[i, :, cols] = total
-
-        @pl.when(s > 0)
-        def _():
-            acc_copy(1, s, -1).start()
+        @pl.when((s < REACH) & (me > s) & ((s == REACH - 1) | last))
+        def _():
+            acc_home(s).start()
+
+        @pl.when(s == 0)
+        def _():
+            dkv[:, :, half:] = later[...]
 
         return 0
 
     lax.fori_loop(0, REACH + 1, step, 0)
-    acc_copy(1, REACH, -1).wait_recv()
+    pass_on(jnp.int32(REACH))
+
+    @pl.when(me < n - 1)
+    def _():
+        acc_copy(1, REACH, -1).wait_recv()
+
     dkv[:, :, half:] += acc_in[1, REACH + 1].astype(F32)
     dq_store.wait()
 
     def drain(s, _):
-        for way in range(2):
-            key_copy(way, REACH, s + way, 1).wait_send()
-            acc_copy(way, s + way, 1).wait_send()
+        @pl.when(((s == 0) | (me >= s)) & (me < n - 1))
+        def _():
+            key_copy(0, REACH, s, 1).wait_send()
+
+        @pl.when(me > s)
+        def _():
+            acc_copy(0, s, 1).wait_send()
+
+        @pl.when((s > 0) & (me >= REACH + 1 - s))
+        def _():
+            key_copy(1, REACH, s + 1, 1).wait_send()
+
+        @pl.when(me >= REACH - s)
+        def _():
+            acc_copy(1, s + 1, 1).wait_send()
+
         return 0
+
+    @pl.when(me < n - REACH)
+    def _():
+        key_copy(1, REACH, 1, 1).wait_send()
+
+    for offset in range(1, REACH):
+
+        @pl.when(me == n - 1 - offset)
+        def _():
+            own_send(REACH + 1 - offset, offset).wait_send()
 
     lax.fori_loop(0, REACH, drain, 0)
 
@@ -279,9 +366,10 @@
             pltpu.VMEM((rows, d), F32),
             pltpu.VMEM((rows, rows), F32),
             full,
-            pltpu.VMEM((REACH + 1, 2, rows, d), BF16),
+            pltpu.VMEM((REACH + 1, 2, 2, half, d), BF16),
             pltpu.VMEM((2, REACH + 2, 2, d, half), BF16),
             pltpu.VMEM((2, REACH + 1, 2, d, half), BF16),
+            pltpu.VMEM((2, d, half), F32),
             pltpu.SemaphoreType.DMA((9,)),
             pltpu.SemaphoreType.DMA,
             copies, copies, copies, copies,

time: 54.7 us -> 53.2 us (0.973)
  the two profiles are of different devices: /device:TPU:62 before, /device:TPU:54 now
where the time goes in v3:
time: 53.2 us; the launch traced here: 53.1 us
  Pallas kernels  52.5 us (99%)
  between operations  0.64 us (1%)
    pallas_call x1, Pallas kernels, on_device(): pl.pallas_call(functools.partial(kernel, n), out_shape=(pltpu.VMEM((rows,...  50.9 us
    pallas_call x1, Pallas kernels, on_device(): pl.pallas_call(finish_kernel, out_shape=(jax.ShapeDtypeStruct((rows, widt...  1.55 us

profile of v3, /device:TPU:54, one launch (start us, length us, event | category | flops | bytes accessed | tf_op | source)
XLA Modules:
  0.0 53.1 jit_solution(3284645753613871231)
XLA Ops:
  0.6 50.9 %shard_map.94 = (f32[256,2048]{1,0:T(8,128)S(1)}, f32[2,128,256]{2,1,0:T(8,128)S(1)}) custom-call(bf16[256,2048]{1,0:T(8,128)(2,1)} %q_hbm.1, bf16[256,128]{1,0:T(8,128)(2,1)} %k_hbm.1, bf16[256,128]{1,0:T(8,128)(2,1)} %v_hbm.1, bf16[256,2048]{1,0:T(8,128)(2,1)} %o_hbm.1, bf16[256,2048]{1,0:T(8,128)(2,1)} %g_hbm.1, f32[16,256]{1,0:T(8,128)} %norm_hbm.1, ...), custom_call_target="tpu_custom_call" | custom-call | tf_op jit(solution)/shard_map/pallas_call | solution.py:356
  51.6 1.6 %shard_map.95 = (f32[256,2048]{1,0:T(8,128)}, f32[256,128]{1,0:T(8,128)}, f32[256,128]{1,0:T(8,128)}) custom-call(f32[256,2048]{1,0:T(8,128)S(1)} %get-tuple-element.5.dq_ref, f32[2,128,256]{2,1,0:T(8,128)S(1)} %get-tuple-element.6.dkv_ref), custom_call_target="tpu_custom_call" | custom-call | tf_op jit(solution)/shard_map/pallas_call | solution.py:383

commit v4 on v3

--- a/solution.py
+++ b/solution.py
@@ -256,15 +256,17 @@
         def _():
             dq_store.start()
 
-        @pl.when((s > 0) & (((s < REACH) & (me > s)) | ((s == REACH) & (me < n - 1))))
+        @pl.when((s > 0) & (s < REACH) & (me > s))
         def _():
             acc_copy(0, s - 1, 1).wait_recv()
 
         for i in range(2):
-            total = sums[i][:, :half] + acc_in[0, s, i].astype(F32)
-            dkv[i, :, :half] = total
-            acc_out[0, s, i] = total.astype(BF16)
+            dkv[i, :, :half] = sums[i][:, :half]
             later[i] = sums[i][:, half:]
+
+        @pl.when(s < REACH)
+        def _():
+            acc_out[0, s] = (dkv[:, :, :half] + acc_in[0, s].astype(F32)).astype(BF16)
 
         @pl.when((s < REACH - 1) & (me > s) & (me < n - 1))
         def _():
@@ -282,6 +284,12 @@
 
     lax.fori_loop(0, REACH + 1, step, 0)
     pass_on(jnp.int32(REACH))
+
+    @pl.when(me < n - 1)
+    def _():
+        acc_copy(0, REACH - 1, 1).wait_recv()
+
+    dkv[:, :, :half] += acc_in[0, REACH].astype(F32)
 
     @pl.when(me < n - 1)
     def _():

time: 53.2 us -> 51.5 us (0.968)
  the two profiles are of different devices: /device:TPU:54 before, /device:TPU:16 now
where the time goes in v4:
time: 51.5 us; the launch traced here: 50.6 us
  Pallas kernels  50 us (97%)
  between operations  0.64 us (1%)
    pallas_call x1, Pallas kernels, on_device(): pl.pallas_call(functools.partial(kernel, n), out_shape=(pltpu.VMEM((rows,...  48.4 us
    pallas_call x1, Pallas kernels, on_device(): pl.pallas_call(finish_kernel, out_shape=(jax.ShapeDtypeStruct((rows, widt...  1.55 us

profile of v4, /device:TPU:16, one launch (start us, length us, event | category | flops | bytes accessed | tf_op | source)
XLA Modules:
  0.0 50.6 jit_solution(17793137580360238303)
XLA Ops:
  0.6 48.4 %shard_map.94 = (f32[256,2048]{1,0:T(8,128)S(1)}, f32[2,128,256]{2,1,0:T(8,128)S(1)}) custom-call(bf16[256,2048]{1,0:T(8,128)(2,1)} %q_hbm.1, bf16[256,128]{1,0:T(8,128)(2,1)} %k_hbm.1, bf16[256,128]{1,0:T(8,128)(2,1)} %v_hbm.1, bf16[256,2048]{1,0:T(8,128)(2,1)} %o_hbm.1, bf16[256,2048]{1,0:T(8,128)(2,1)} %g_hbm.1, f32[16,256]{1,0:T(8,128)} %norm_hbm.1, ...), custom_call_target="tpu_custom_call" | custom-call | tf_op jit(solution)/shard_map/pallas_call | solution.py:364
  49.1 1.6 %shard_map.95 = (f32[256,2048]{1,0:T(8,128)}, f32[256,128]{1,0:T(8,128)}, f32[256,128]{1,0:T(8,128)}) custom-call(f32[256,2048]{1,0:T(8,128)S(1)} %get-tuple-element.5.dq_ref, f32[2,128,256]{2,1,0:T(8,128)S(1)} %get-tuple-element.6.dkv_ref), custom_call_target="tpu_custom_call" | custom-call | tf_op jit(solution)/shard_map/pallas_call | solution.py:391

commit v5 on v4

--- a/solution.py
+++ b/solution.py
@@ -252,10 +252,6 @@
             dq[:, cols] += dot(score_grad, k)
         sums = (dk, dv)
 
-        @pl.when(s == REACH)
-        def _():
-            dq_store.start()
-
         @pl.when((s > 0) & (s < REACH) & (me > s))
         def _():
             acc_copy(0, s - 1, 1).wait_recv()
@@ -284,6 +280,8 @@
 
     lax.fori_loop(0, REACH + 1, step, 0)
     pass_on(jnp.int32(REACH))
+    dq[...] = dq[...] * d**-0.5
+    dq_store.start()
 
     @pl.when(me < n - 1)
     def _():
@@ -330,22 +328,19 @@
     lax.fori_loop(0, REACH, drain, 0)
 
 
-def finish_kernel(dq_ref, dkv_ref, dq_hbm, dk_hbm, dv_hbm, dq, dk, dv, sems):
-    rows, width = dq.shape
+def finish_kernel(dq_ref, dkv_ref, dq_hbm, dk_hbm, dv_hbm, dk, dv, sems):
+    rows = dq_ref.shape[0]
     factor = dk.shape[1] ** -0.5
+    part = rows // 4
+    copies = []
+    for i in range(4):
+        here = pl.ds(i * part, part)
+        copies.append(pltpu.make_async_copy(dq_ref.at[here], dq_hbm.at[here], sems.at[2 + i]))
+        copies[-1].start()
     dk[...] = dkv_ref[0].T * factor
     dv[...] = dkv_ref[1].T
-    copies = [
-        pltpu.make_async_copy(dk, dk_hbm, sems.at[0]),
-        pltpu.make_async_copy(dv, dv_hbm, sems.at[1]),
-    ]
-    for c in copies:
-        c.start()
-    part = rows // 4
-    for i in range(4):
-        here = pl.ds(i * part, part)
-        dq[here, :] = dq_ref[here, :] * factor
-        copies.append(pltpu.make_async_copy(dq.at[here], dq_hbm.at[here], sems.at[2 + i]))
+    for i, (src, dst) in enumerate(((dk, dk_hbm), (dv, dv_hbm))):
+        copies.append(pltpu.make_async_copy(src, dst, sems.at[i]))
         copies[-1].start()
     for c in copies:
         c.wait()
@@ -394,7 +389,6 @@
         in_specs=[whole, whole],
         out_specs=(anywhere,) * 3,
         scratch_shapes=[
-            full,
             pltpu.VMEM((rows, d), F32),
             pltpu.VMEM((rows, d), F32),
             pltpu.SemaphoreType.DMA((6,)),

time: 51.5 us -> 51.4 us (level)
  no operation moved by 1% of the time
where the time goes in v5:
time: 51.4 us; the launch traced here: 50.5 us
  Pallas kernels  49.9 us (97%)
  between operations  0.64 us (1%)
    pallas_call x1, Pallas kernels, on_device(): pl.pallas_call(functools.partial(kernel, n), out_shape=(pltpu.VMEM((rows,...  48.4 us
    pallas_call x1, Pallas kernels, on_device(): pl.pallas_call(finish_kernel, out_shape=(jax.ShapeDtypeStruct((rows, widt...  1.44 us

profile of v5, /device:TPU:16, one launch (start us, length us, event | category | flops | bytes accessed | tf_op | source)
XLA Modules:
  0.0 50.5 jit_solution(6145560098348098710)
XLA Ops:
  0.6 48.4 %shard_map.94 = (f32[256,2048]{1,0:T(8,128)S(1)}, f32[2,128,256]{2,1,0:T(8,128)S(1)}) custom-call(bf16[256,2048]{1,0:T(8,128)(2,1)} %q_hbm.1, bf16[256,128]{1,0:T(8,128)(2,1)} %k_hbm.1, bf16[256,128]{1,0:T(8,128)(2,1)} %v_hbm.1, bf16[256,2048]{1,0:T(8,128)(2,1)} %o_hbm.1, bf16[256,2048]{1,0:T(8,128)(2,1)} %g_hbm.1, f32[16,256]{1,0:T(8,128)} %norm_hbm.1, ...), custom_call_target="tpu_custom_call" | custom-call | tf_op jit(solution)/shard_map/pallas_call | solution.py:359
  49.1 1.4 %shard_map.95 = (f32[256,2048]{1,0:T(8,128)}, f32[256,128]{1,0:T(8,128)}, f32[256,128]{1,0:T(8,128)}) custom-call(f32[256,2048]{1,0:T(8,128)S(1)} %get-tuple-element.5.dq_ref, f32[2,128,256]{2,1,0:T(8,128)S(1)} %get-tuple-element.6.dkv_ref), custom_call_target="tpu_custom_call" | custom-call | tf_op jit(solution)/shard_map/pallas_call | solution.py:386
